TPU v7x, 32 devices: a whole 2x2x4 slice. The times are simulated.
32 devices in a mesh: ctx: 8 (over z, x), head: 4 (over y, core).
Axes of the slice: x: 2, y: 2, z: 4, core: 2. Of those that a mesh axis runs over, the one named last changes fastest.
Arguments:
- queries: bfloat16 [512, 8192], P('ctx', 'head'), may hold values from -6 to 6
- keys: bfloat16 [512, 128], P('ctx'), may hold values from -6 to 6
- key_gain: float32 [128], replicated, may hold values from 0.25 to 1.75
- key_bias: float32 [128], replicated, may hold values from -0.5 to 0.5
- head_weights: bfloat16 [512, 64], P('ctx', 'head'), may hold values from -6 to 6
- positions: int32 [512], P('ctx'), may hold values from 0 to 383, as said below
Outputs:
- index_scores: float32 [512, 512], P(('ctx', 'head'))
Inputs may be any that keep to these rules, and one draw needn't show every extreme that they name: `positions`: positions of packed documents: the first 384 tokens form one document and the rest is split into one to three documents at drawn points; a token's position counts from its document's first token.
All inputs are finite; a program needn't handle non-finite values.
Results may differ from a plain program's by a relative error of at most 0.0095.
Values may be sent and summed in bfloat16 or wider, within the bound.
A program may use at most 64 MiB of HBM per device.

v0:
```python
import math

import jax
import jax.numpy as jnp
import numpy as np
from jax import lax
from jax.sharding import PartitionSpec as P

H = 64
DH = 128
ROPE = 64


def yarn_frequencies(rope_dims):
    half_dims = rope_dims // 2
    exponent = np.arange(0, rope_dims, 2) / rope_dims
    extra_freq = 1.0 / 10000.0**exponent
    inter_freq = extra_freq / 40.0

    def correction(beta):
        return rope_dims * math.log(4096.0 / (beta * 2.0 * math.pi)) / (2.0 * math.log(10000.0))

    low_dim = max(math.floor(correction(32.0)), 0)
    high_dim = min(math.ceil(correction(1.0)), rope_dims - 1)
    ramp_values = np.clip((np.arange(half_dims) - low_dim) / (high_dim - low_dim), 0.0, 1.0)
    return (inter_freq * ramp_values + extra_freq * (1.0 - ramp_values)).astype(np.float32)


def rotate(values, angles):
    half_rope = ROPE // 2
    cosine = jnp.cos(angles)[:, None, :]
    sine = jnp.sin(angles)[:, None, :]
    first = values[..., :half_rope]
    second = values[..., half_rope:ROPE]
    return jnp.concatenate(
        [first * cosine - second * sine, second * cosine + first * sine, values[..., ROPE:]], -1
    )


def key_norm(keys, key_gain, key_bias):
    values = keys.astype(jnp.float32)
    centered = values - jnp.mean(values, axis=-1, keepdims=True)
    spread = jnp.mean(centered * centered, axis=-1, keepdims=True)
    return centered * lax.rsqrt(spread + 1e-06) * key_gain + key_bias


def tile_scores(q_block, weights, k_block, groups, row_glob, row_doc, key_glob):
    rows_here = q_block.shape[0]
    heads_here = weights.shape[1]
    raw = lax.dot_general(
        q_block.reshape(rows_here * heads_here, DH),
        k_block,
        (((1,), (1,)), ((), ())),
        preferred_element_type=jnp.float32,
    )
    active = jnp.maximum(raw, 0.0).reshape(
        rows_here, groups, heads_here // groups, k_block.shape[0]
    )
    partial_sum = jnp.sum(
        active * weights.reshape(rows_here, groups, heads_here // groups, 1), axis=2
    )
    visible = (key_glob[None, :] >= row_doc[:, None]) & (key_glob[None, :] <= row_glob[:, None])
    partial_sum = jnp.where(visible[:, None, :], partial_sum, jnp.zeros_like(partial_sum))
    return partial_sum.astype(jnp.bfloat16)


def on_device(queries, keys, key_gain, key_bias, head_weights, positions):
    tok_rows = queries.shape[0]
    local_heads = queries.shape[1] // DH
    ctx_rank = lax.axis_index("ctx")
    freqs = jnp.asarray(yarn_frequencies(ROPE))
    angles = positions.astype(jnp.float32)[:, None] * freqs[None, :]
    q_rot = (
        rotate(queries.astype(jnp.float32).reshape(tok_rows, local_heads, DH), angles)
        .reshape(tok_rows, local_heads * DH)
        .astype(jnp.bfloat16)
    )
    k_rot = (
        rotate(key_norm(keys, key_gain, key_bias)[:, None, :], angles)
        .reshape(tok_rows, DH)
        .astype(jnp.bfloat16)
    )
    scale = 1.0 / math.sqrt(H * DH)
    groups = lax.axis_size("head")
    head_rank = lax.axis_index("head")
    rows_each = tok_rows // groups
    rows_q, w_moved = (
        lax.all_to_all(q_rot, "head", split_axis=0, concat_axis=1, tiled=True),
        lax.all_to_all(head_weights, "head", split_axis=0, concat_axis=1, tiled=True),
    )
    rows_w = w_moved.astype(jnp.float32) * scale
    row_first = head_rank * rows_each
    row_glob = ctx_rank * tok_rows + row_first + jnp.arange(rows_each, dtype=jnp.int32)
    row_doc = row_glob - lax.dynamic_slice_in_dim(positions, row_first, rows_each, 0)
    rows_here = rows_q.shape[0]
    out_type = jnp.float32
    row_last = jnp.max(row_glob)
    doc_first = jnp.min(row_doc)

    def score_block(k_block, key_glob):
        parts = tile_scores(rows_q, rows_w, k_block, groups, row_glob, row_doc, key_glob)
        return jnp.sum(parts.astype(jnp.float32), axis=1)

    piece = lax.all_gather(k_rot, "ctx", axis=0, tiled=True)
    start = jnp.int32(0)
    piece_len = piece.shape[0]
    block_len = math.gcd(piece_len, 512)
    count = piece_len // block_len

    def compute(operand):
        if count == 1:
            return score_block(piece, start + jnp.arange(piece_len, dtype=jnp.int32))
        stacked = piece.reshape(count, block_len, DH)
        offsets = start + block_len * jnp.arange(count, dtype=jnp.int32)

        def one_block(inputs):
            k_block, offset = inputs
            return score_block(k_block, offset + jnp.arange(block_len, dtype=jnp.int32))

        tiles = lax.map(one_block, (stacked, offsets))
        return jnp.transpose(tiles, (1, 0, 2)).reshape(rows_here, piece_len)

    def skip(operand):
        return jnp.zeros((rows_here, piece_len), out_type)

    live = (start <= row_last) & (start + piece_len > doc_first)
    return lax.cond(live, compute, skip, 0)


def solution(mesh):
    in_specs = (P("ctx", "head"), P("ctx", None), P(), P(), P("ctx", "head"), P("ctx"))
    out_specs = P(("ctx", "head"), None)
    return jax.shard_map(
        on_device, mesh=mesh, in_specs=in_specs, out_specs=out_specs, check_vma=False
    )
```

profile of v0, /device:TPU:0, one launch (start us, length us, event | category | flops | bytes accessed | tf_op | source)
XLA Modules:
  0.0 57.5 jit_solution(6906235586217936700)
XLA Ops:
  0.0 0.0 copy-start
  0.0 0.8 %all_to_all.28 = bf16[4,16,16]{1,0,2:T(4,128)(2,1)S(1)} reshape(bf16[64,16]{0,1:T(8,128)(2,1)} %param.13) | data formatting | bytes 4096 | tf_op jit(solution)/shard_map/all_to_all | solution.py:89
  0.8 0.7 %reshape.171 = bf16[4,2,128]{2,1,0:T(2,128)(2,1)} reshape(bf16[4,16,16]{2,1,0:T(8,128)(2,1)S(1)} %bitcast.24) | data formatting | bytes 4096
  1.5 4.2 %all-to-all-start.1 = ((bf16[4,2,128]{2,1,0:T(2,128)(2,1)}), bf16[4,2,128]{2,1,0:T(2,128)(2,1)S(1)}, u32[]{:S(2)}, u32[]{:S(2)}) async-start(bf16[4,2,128]{2,1,0:T(2,128)(2,1)} %reshape.171), calls=%async_computation.1 | async-start | bytes 4096 | tf_op jit(solution)/shard_map/all_to_all | solution.py:89
  5.7 0.7 %convert_element_type.34 = f32[64]{0:T(128)S(1)} convert(s32[64]{0:T(128)} %param.14) | non-fusion elementwise | flops 64 | bytes 512 | tf_op jit(solution)/shard_map/convert_element_type | solution.py:72
  6.4 0.8 %copy.29 = bf16[64,128]{0,1:T(8,128)(2,1)S(1)} copy(bf16[64,128]{1,0:T(8,128)(2,1)} %param.10) | data formatting | bytes 32768 | tf_op args[1]
  7.3 0.8 %fusion.6 = f32[64,1,128]{0,2,1:T(8,128)S(1)} fusion(bf16[64,128]{0,1:T(8,128)(2,1)S(1)} %copy.29, f32[128]{0:T(128)} %param.12, f32[128]{0:T(128)} %param.11, f32[64]{0:T(128)S(1)} %add_rsqrt_fusion, f32[64]{0:T(128)S(1)} %broadcast_multiply_fusion), kind=kLoop, calls=%fused_computation.18 | loop fusion | flops 40960 | bytes 50688 | tf_op jit(solution)/shard_map/broadcast_in_dim | solution.py:79
  8.1 0.9 %multiply_cosine_fusion = (f32[64,32]{1,0:T(8,128)S(1)}, f32[64,32]{1,0:T(8,128)S(1)}) fusion(f32[32]{0:T(128)} %constant.42.clone, f32[64]{0:T(128)S(1)} %convert_element_type.34), kind=kLoop, calls=%fused_computation.20 | loop fusion | flops 2048 | bytes 16768 | tf_op jit(solution)/shard_map/cos | solution.py:31
  9.0 0.8 %fusion.12 = (bf16[64,1,32]{0,2,1:T(8,128)(2,1)S(1)}, bf16[64,1,32]{0,2,1:T(8,128)(2,1)S(1)}) fusion(f32[64,1,128]{0,2,1:T(8,128)S(1)} %fusion.6, f32[32]{0:T(128)} %constant.42.clone, f32[64]{0:T(128)S(1)} %convert_element_type.34), kind=kLoop, calls=%fused_computation.30 | loop fusion | flops 18432 | bytes 24960 | tf_op jit(solution)/shard_map/convert.1
  9.8 1.4 %fusion.16 = (s32[]{:T(128)}, s32[16]{0:T(128)S(1)}) fusion(s32[64]{0:T(128)} %param.14, s32[]{:T(128)S(6)} %select_n.8, s32[]{:T(128)S(6)} %add.37), kind=kLoop, calls=%fused_computation.39 | loop fusion | flops 47 | bytes 140 | tf_op jit(solution)/shard_map/reduce_min | solution.py:98
  11.2 0.0 copy-done
  11.3 0.1 bitcast_convert_fusion
  11.3 0.1 slice.28
  11.5 0.1 copy.30
  11.6 0.2 subtract_convert_fusion
  11.8 0.3 pad_maximum_fusion
  12.1 31.4 %all-gather = bf16[512,1,128]{2,0,1:T(8,128)(2,1)S(1)} all-gather(bf16[64,1,128]{2,0,1:T(8,128)(2,1)S(1)} %copy.30), channel_id=2, replica_groups=mesh['ctx'=8,'head'=4] {'ctx'}, dimensions={0}, use_global_device_ids=true | all-gather | bytes 147456 | tf_op jit(solution)/shard_map/all_gather | solution.py:104
  43.5 0.6 %fusion.15 = s32[]{:T(128)} fusion(s32[]{:T(128)S(6)} %add.37), kind=kLoop, calls=%fused_computation.38 | loop fusion | flops 31 | bytes 8 | tf_op jit(solution)/shard_map/reduce_max | solution.py:97
  45.4 0.8 %convert_element_type.35 = bf16[4,16,2048]{2,1,0:T(8,128)(2,1)} reshape(bf16[64,16,128]{2,1,0:T(8,128)(2,1)S(1)} %pad_maximum_fusion) | data formatting | bytes 524288 | tf_op jit(solution)/shard_map/convert_element_type | solution.py:76
  46.2 0.0 all-to-all-done.1
  46.2 3.4 %all-to-all-start = ((bf16[4,16,2048]{2,1,0:T(8,128)(2,1)}), bf16[4,16,2048]{2,1,0:T(8,128)(2,1)S(1)}, u32[]{:S(2)}, u32[]{:S(2)}) async-start(bf16[4,16,2048]{2,1,0:T(8,128)(2,1)} %convert_element_type.35), calls=%async_computation | async-start | bytes 524288 | tf_op jit(solution)/shard_map/all_to_all | solution.py:88
  49.6 0.1 reshape.172
  49.7 5.9 %all-to-all-done = bf16[4,16,2048]{2,1,0:T(8,128)(2,1)S(1)} async-done(((bf16[4,16,2048]{2,1,0:T(8,128)(2,1)}), bf16[4,16,2048]{2,1,0:T(8,128)(2,1)S(1)}, u32[]{:S(2)}, u32[]{:S(2)}) %all-to-all-start) | async-done | bytes 262176 | tf_op jit(solution)/shard_map/all_to_all | solution.py:88
  55.6 1.3 %conditional.1 = (f32[16,512]{1,0:T(8,128)S(1)}) conditional(s32[]{:T(128)} %convert_element_type.33, () %tuple.14, (s32[16]{0:T(128)S(1)}, s32[16]{0:T(128)S(1)}, bf16[16,4,2048]{2,0,1:T(8,128)(2,1)S(1)}, bf16[512,128]{1,0:T(8,128)(2,1)S(1)}, bf16[16,4,16]{0,2,1:T(8,128)(2,1)S(1)}) %tuple.31), branch_computations={%region_4.0_spmd, %region_5.8_spmd} | conditional | flops 135874560 | bytes 1636488 | solution.py:127
  55.6 0.1 copy.33
  55.7 0.2 copy.32
  55.9 0.2 reshape.163
  56.1 0.6 %multiply_reduce_fusion = bf16[16,4,512]{2,1,0:T(4,128)(2,1)S(1)} fusion(f32[16,4,16]{2,1,0:T(4,128)S(1)} %convert_multiply_fusion, bf16[1024,128]{1,0:T(8,128)(2,1)S(1)} %reshape.163, bf16[512,128]{1,0:T(8,128)(2,1)S(1)} %get-tuple-element.37), kind=kOutput, calls=%fused_computation | convolution fusion | flops 135757824 | bytes 462848 | tf_op jit(solution)/shard_map/cond/branch_1_fun/dot_general | solution.py:50
  56.7 0.1 fusion
  56.8 0.1 convert_reduce_fusion
  56.9 0.0 copy-start.1
  56.9 0.6 %copy-done.1 = f32[16,512]{1,0:T(8,128)} copy-done((f32[16,512]{1,0:T(8,128)}, f32[16,512]{1,0:T(8,128)S(1)}, u32[]{:S(2)}) %copy-start.1) | copy-done | bytes 32792
  (11 shorter events, 0.2 us)
Async XLA Ops:
  0.0 11.2 %copy-start = (bf16[64,2048]{1,0:T(8,128)(2,1)S(1)}, bf16[64,2048]{1,0:T(8,128)(2,1)}, u32[]{:S(2)}) copy-start(bf16[64,2048]{1,0:T(8,128)(2,1)} %param.9) | copy-start | bytes 786436
  1.5 44.7 %all-to-all-start.1 = ((bf16[4,2,128]{2,1,0:T(2,128)(2,1)}), bf16[4,2,128]{2,1,0:T(2,128)(2,1)S(1)}, u32[]{:S(2)}, u32[]{:S(2)}) async-start(bf16[4,2,128]{2,1,0:T(2,128)(2,1)} %reshape.171), calls=%async_computation.1 | async-start | bytes 4096 | tf_op jit(solution)/shard_map/all_to_all | solution.py:89
  46.2 9.4 %all-to-all-start = ((bf16[4,16,2048]{2,1,0:T(8,128)(2,1)}), bf16[4,16,2048]{2,1,0:T(8,128)(2,1)S(1)}, u32[]{:S(2)}, u32[]{:S(2)}) async-start(bf16[4,16,2048]{2,1,0:T(8,128)(2,1)} %convert_element_type.35), calls=%async_computation | async-start | bytes 524288 | tf_op jit(solution)/shard_map/all_to_all | solution.py:88
  56.9 0.6 %copy-start.1 = (f32[16,512]{1,0:T(8,128)}, f32[16,512]{1,0:T(8,128)S(1)}, u32[]{:S(2)}) copy-start(f32[16,512]{1,0:T(8,128)S(1)} %get-tuple-element.81) | copy-start | bytes 98308
where the time goes:
time: 58 us; the launch traced here: 57.5 us
  blocking collectives  31.4 us (54%)
  starting transfers between devices  7.64 us (13%)
  other arithmetic  6.02 us (10%)
  waiting for transfers between devices  5.92 us (10%)
  local copies, waits for them, and re-layouts  4.55 us (8%)
  between operations  1.37 us (2%)
  matrix products  0.63 us (1%)
    all_gather x1, blocking collectives, on_device(): piece = lax.all_gather(k_rot, 'ctx', axis=0, tiled=True)  31.4 us
    all_to_all x1, waiting for transfers between devices, on_device(): lax.all_to_all(q_rot, 'head', split_axis=0, concat_axis=1, tiled=True)  5.92 us
    all_to_all x1, starting transfers between devices, on_device(): lax.all_to_all(head_weights, 'head', split_axis=0, concat_axis=1, tiled=T...  4.24 us
    all_to_all x1, starting transfers between devices, on_device(): lax.all_to_all(q_rot, 'head', split_axis=0, concat_axis=1, tiled=True)  3.41 us
    unnamed x8, local copies, waits for them, and re-layouts  2.23 us
    reduce_min x1, other arithmetic, on_device(): doc_first = jnp.min(row_doc)  1.45 us
  transfers between devices with their start and end apart: 2, of which 1 were waited for; matrix products, arithmetic and copies ran while one was open for 14% of the time, Pallas kernels for 0%

commit v1 on v0

v1 whole, which is shorter than its diff:
```python
import functools
import math

import jax
import jax.numpy as jnp
import numpy as np
from jax import lax
from jax.experimental import pallas as pl
from jax.experimental.pallas import tpu as pltpu
from jax.sharding import PartitionSpec as P

H = 64
DH = 128
ROPE = 64
MESH = pl.DeviceIdType.MESH


def yarn_frequencies(rope_dims):
    half_dims = rope_dims // 2
    exponent = np.arange(0, rope_dims, 2) / rope_dims
    extra_freq = 1.0 / 10000.0**exponent
    inter_freq = extra_freq / 40.0

    def correction(beta):
        return rope_dims * math.log(4096.0 / (beta * 2.0 * math.pi)) / (2.0 * math.log(10000.0))

    low_dim = max(math.floor(correction(32.0)), 0)
    high_dim = min(math.ceil(correction(1.0)), rope_dims - 1)
    ramp_values = np.clip((np.arange(half_dims) - low_dim) / (high_dim - low_dim), 0.0, 1.0)
    return (inter_freq * ramp_values + extra_freq * (1.0 - ramp_values)).astype(np.float32)


def sin_cos(angle):
    turns = jnp.floor(angle * (2.0 / math.pi) + 0.5)
    rest = angle - turns * 1.5703125
    rest = rest - turns * 4.837512969970703125e-4
    rest = rest - turns * 7.54978995489188216e-8
    square = rest * rest
    sine = ((-1.9515295891e-4 * square + 8.3321608736e-3) * square - 1.6666654611e-1) * (
        square * rest
    ) + rest
    cosine = (
        ((2.443315711809948e-5 * square - 1.388731625493765e-3) * square + 4.166664568298827e-2)
        * (square * square)
        - 0.5 * square
        + 1.0
    )
    quadrant = turns.astype(jnp.int32)
    odd = (quadrant & 1) == 1
    sine_out = jnp.where(odd, cosine, sine)
    cosine_out = jnp.where(odd, sine, cosine)
    sine_out = jnp.where((quadrant & 2) == 2, -sine_out, sine_out)
    cosine_out = jnp.where(((quadrant + 1) & 2) == 2, -cosine_out, cosine_out)
    return sine_out, cosine_out


def kernel(
    n_ctx,
    n_head,
    chunk,
    queries_hbm,
    keys_hbm,
    gain_hbm,
    bias_hbm,
    weights_hbm,
    positions_hbm,
    freq_hbm,
    out_ref,
    q_in,
    k_in,
    gain_in,
    bias_in,
    w_in,
    pos_in,
    freq_in,
    q_rot,
    w_wide,
    k_all,
    part_out,
    part_in,
    in_sem,
    key_send,
    key_recv,
    part_send,
    part_recv,
):
    c = lax.axis_index("ctx")
    g = lax.axis_index("head")
    rows = q_in.shape[0]
    heads = q_in.shape[1] // DH
    rows_each = rows // n_head
    tokens = n_ctx * rows
    first_end = 3 * tokens // 4
    late = c * rows >= first_end
    src_first = jnp.where(late, first_end // rows, 0)
    crossing = (c + 1) * rows > first_end
    dst_end = jnp.where(crossing, n_ctx, -(-first_end // rows))

    barrier = pltpu.get_barrier_semaphore()

    def greet(i, carry):
        pl.semaphore_signal(barrier, inc=1, device_id={"ctx": i, "head": g}, device_id_type=MESH)
        return carry

    lax.fori_loop(src_first, c, greet, 0)
    for d in range(1, n_head):
        pl.semaphore_signal(
            barrier,
            inc=1,
            device_id={"ctx": c, "head": lax.rem(g + d, n_head)},
            device_id_type=MESH,
        )

    copies = [
        pltpu.make_async_copy(src, dst, in_sem.at[i])
        for i, (src, dst) in enumerate(
            [
                (positions_hbm, pos_in),
                (freq_hbm, freq_in),
                (keys_hbm, k_in),
                (gain_hbm, gain_in),
                (bias_hbm, bias_in),
                (weights_hbm, w_in),
                (queries_hbm, q_in),
            ]
        )
    ]
    for copy in copies:
        copy.start()
    out_ref[...] = jnp.zeros_like(out_ref)

    copies[0].wait()
    copies[1].wait()
    pos_wide = jnp.broadcast_to(pos_in[...].reshape(1, rows).astype(jnp.float32), (rows, rows))
    here = lax.broadcasted_iota(jnp.int32, (rows, rows), 0)
    there = lax.broadcasted_iota(jnp.int32, (rows, rows), 1)
    pos = jnp.sum(jnp.where(here == there, pos_wide, 0.0), axis=1, keepdims=True)
    sine, cosine = sin_cos(pos * freq_in[...])
    lane = lax.broadcasted_iota(jnp.int32, (rows, DH), 1)
    half = ROPE // 2
    sine_low = jnp.where(lane < half, -sine, 0.0)
    sine_high = jnp.where((lane >= half) & (lane < ROPE), sine, 0.0)

    def rotate(values):
        return (
            values * cosine
            + pltpu.roll(values, DH - half, 1) * sine_low
            + pltpu.roll(values, half, 1) * sine_high
        )

    for copy in copies[2:5]:
        copy.wait()
    values = k_in[...].astype(jnp.float32)
    centered = values - jnp.mean(values, axis=-1, keepdims=True)
    spread = jnp.mean(centered * centered, axis=-1, keepdims=True)
    normed = centered * lax.rsqrt(spread + 1e-06) * gain_in[...].reshape(1, DH) + bias_in[
        ...
    ].reshape(1, DH)
    mine = pl.ds(pl.multiple_of(c * rows, rows), rows)
    k_all[mine, :] = rotate(normed).astype(jnp.bfloat16)

    pl.semaphore_wait(barrier, dst_end - c - 1 + n_head - 1)

    def key_copy(owner, target):
        place = pl.ds(pl.multiple_of(owner * rows, rows), rows)
        return pltpu.make_async_remote_copy(
            src_ref=k_all.at[place],
            dst_ref=k_all.at[place],
            send_sem=key_send.at[target],
            recv_sem=key_recv.at[owner],
            device_id={"ctx": target, "head": g},
            device_id_type=MESH,
        )

    def send_keys(i, carry):
        key_copy(c, dst_end + c - i).start()
        return carry

    lax.fori_loop(c + 1, dst_end, send_keys, 0)

    copies[5].wait()
    copies[6].wait()
    scale = 1.0 / math.sqrt(H * DH)
    for h in range(heads):
        q_rot[h * rows : (h + 1) * rows, :] = rotate(
            q_in[:, h * DH : (h + 1) * DH].astype(jnp.float32)
        ).astype(jnp.bfloat16)
        w_wide[h] = jnp.broadcast_to(w_in[:, h : h + 1].astype(jnp.float32) * scale, (rows, DH))

    row_glob = c * rows + lax.broadcasted_iota(jnp.int32, (rows, 1), 0)
    row_doc = row_glob - pos.astype(jnp.int32)
    per_chunk = chunk // rows
    chunk_first = src_first // per_chunk
    chunk_end = c // per_chunk + 1

    def part_copy(t, d):
        peer = lax.rem(g + d, n_head)
        return pltpu.make_async_remote_copy(
            src_ref=part_out.at[t, peer],
            dst_ref=part_in.at[t, d - 1],
            send_sem=part_send.at[t, d - 1],
            recv_sem=part_recv.at[t, d - 1],
            device_id={"ctx": c, "head": peer},
            device_id_type=MESH,
        )

    def score(t, carry):
        def arrive(i, carry):
            key_copy(i, c).wait_recv()
            return carry

        lax.fori_loop(
            jnp.maximum(src_first, t * per_chunk),
            jnp.minimum(c, (t + 1) * per_chunk),
            arrive,
            0,
        )
        first = pl.multiple_of(t * chunk, chunk)
        raw = lax.dot_general(
            q_rot[...],
            k_all[pl.ds(first, chunk), :],
            (((1,), (1,)), ((), ())),
            preferred_element_type=jnp.float32,
        )
        total = jnp.zeros((rows, chunk), jnp.float32)
        for h in range(heads):
            weight = w_wide[h]
            if chunk > DH:
                weight = jnp.concatenate([weight] * (chunk // DH), axis=1)
            total += jnp.maximum(raw[h * rows : (h + 1) * rows, :], 0.0) * weight
        key_glob = first + lax.broadcasted_iota(jnp.int32, (rows, chunk), 1)
        visible = (key_glob >= row_doc) & (key_glob <= row_glob)
        part = jnp.where(visible, total, 0.0).astype(jnp.bfloat16)
        for h in range(n_head):
            part_out[t, h] = part[h * rows_each : (h + 1) * rows_each, :]
        for d in range(1, n_head):
            part_copy(t, d).start()
        return carry

    lax.fori_loop(chunk_first, chunk_end, score, 0)

    def gather(t, carry):
        total = part_out[t, g].astype(jnp.float32)
        for d in range(1, n_head):
            part_copy(t, d).wait_recv()
            total += part_in[t, d - 1].astype(jnp.float32)
        out_ref[:, pl.ds(pl.multiple_of(t * chunk, chunk), chunk)] = total
        return carry

    lax.fori_loop(chunk_first, chunk_end, gather, 0)

    def sent_keys(i, carry):
        key_copy(c, i).wait_send()
        return carry

    lax.fori_loop(c + 1, dst_end, sent_keys, 0)

    def sent_parts(t, carry):
        for d in range(1, n_head):
            part_copy(t, d).wait_send()
        return carry

    lax.fori_loop(chunk_first, chunk_end, sent_parts, 0)


def solution(mesh):
    n_ctx, n_head = mesh.shape["ctx"], mesh.shape["head"]
    freqs = yarn_frequencies(ROPE)
    freq_wide = np.concatenate([freqs, freqs, np.zeros(DH - ROPE, np.float32)])[None, :]

    def on_device(queries, keys, key_gain, key_bias, head_weights, positions):
        rows = queries.shape[0]
        heads = queries.shape[1] // DH
        tokens = n_ctx * rows
        chunk = max(DH, tokens // 16)
        n_chunk = tokens // chunk
        rows_each = rows // n_head
        return pl.pallas_call(
            functools.partial(kernel, n_ctx, n_head, chunk),
            out_shape=jax.ShapeDtypeStruct((rows_each, tokens), jnp.float32),
            in_specs=[pl.BlockSpec(memory_space=pl.ANY)] * 7,
            out_specs=pl.BlockSpec(memory_space=pltpu.VMEM),
            scratch_shapes=[
                pltpu.VMEM(queries.shape, jnp.bfloat16),
                pltpu.VMEM(keys.shape, jnp.bfloat16),
                pltpu.VMEM(key_gain.shape, jnp.float32),
                pltpu.VMEM(key_bias.shape, jnp.float32),
                pltpu.VMEM(head_weights.shape, jnp.bfloat16),
                pltpu.VMEM(positions.shape, jnp.int32),
                pltpu.VMEM((1, DH), jnp.float32),
                pltpu.VMEM((heads * rows, DH), jnp.bfloat16),
                pltpu.VMEM((heads, rows, DH), jnp.float32),
                pltpu.VMEM((tokens, DH), jnp.bfloat16),
                pltpu.VMEM((n_chunk, n_head, rows_each, chunk), jnp.bfloat16),
                pltpu.VMEM((n_chunk, n_head - 1, rows_each, chunk), jnp.bfloat16),
                pltpu.SemaphoreType.DMA((7,)),
                pltpu.SemaphoreType.DMA((n_ctx,)),
                pltpu.SemaphoreType.DMA((n_ctx,)),
                pltpu.SemaphoreType.DMA((n_chunk, n_head - 1)),
                pltpu.SemaphoreType.DMA((n_chunk, n_head - 1)),
            ],
            compiler_params=pltpu.CompilerParams(
                collective_id=0, has_side_effects=True, vmem_limit_bytes=32 * 1024 * 1024
            ),
        )(queries, keys, key_gain, key_bias, head_weights, positions, jnp.asarray(freq_wide))

    in_specs = (P("ctx", "head"), P("ctx", None), P(), P(), P("ctx", "head"), P("ctx"))
    out_specs = P(("ctx", "head"), None)
    return jax.shard_map(
        on_device, mesh=mesh, in_specs=in_specs, out_specs=out_specs, check_vma=False
    )
```

time: 58 us -> 13.2 us (0.23)
  the two profiles are of different devices: /device:TPU:0 before, /device:TPU:9 now
where the time goes in v1:
time: 13.2 us; the launch traced here: 13 us
  Pallas kernels  10.5 us (80%)
  local copies, waits for them, and re-layouts  2.41 us (18%)
    pallas_call x1, Pallas kernels, on_device(): pl.pallas_call(functools.partial(kernel, n_ctx, n_head, chunk), out_shape...  10.5 us
    unnamed x14, local copies, waits for them, and re-layouts  2.41 us

profile of v1, /device:TPU:9, one launch (start us, length us, event | category | flops | bytes accessed | tf_op | source)
XLA Modules:
  0.0 13.0 jit_solution(5457100480063104533)
XLA Ops:
  0.0 0.0 copy-start.5
  0.0 0.0 copy-start.4
  0.0 0.0 copy-start.3
  0.0 0.0 copy-start.2
  0.0 0.0 copy-start.1
  0.0 0.8 %copy.8.weights_hbm = bf16[64,16]{1,0:T(8,128)(2,1)S(1)} copy(bf16[64,16]{0,1:T(8,128)(2,1)} %param.11) | data formatting | bytes 4096 | tf_op args[4]
  0.9 0.0 copy-done.5
  0.9 0.0 copy-done.4
  0.9 0.0 copy-done.3
  0.9 0.0 copy-done.2
  0.9 0.0 copy-done.1
  0.9 0.0 copy-start
  0.9 0.9 %copy-done = bf16[64,2048]{1,0:T(8,128)(2,1)S(1)} copy-done((bf16[64,2048]{1,0:T(8,128)(2,1)S(1)}, bf16[64,2048]{1,0:T(8,128)(2,1)}, u32[]{:S(2)}) %copy-start) | copy-done | bytes 262168
  1.9 10.5 %shard_map.73 = f32[16,512]{1,0:T(8,128)S(1)} custom-call(bf16[64,2048]{1,0:T(8,128)(2,1)S(1)} %copy-done, bf16[64,128]{1,0:T(8,128)(2,1)S(1)} %copy-done.1, f32[128]{0:T(128)S(1)} %copy-done.2, f32[128]{0:T(128)S(1)} %copy-done.3, bf16[64,16]{1,0:T(8,128)(2,1)S(1)} %copy.8.weights_hbm, s32[64]{0:T(128)S(1)} %copy-done.4, f32[1,128]{1,0:T(1,128)S(1)} %copy-done.5), custom_call_target="tpu_custom_call" | custom-call | tf_op jit(solution)/shard_map/pallas_call | solution.py:278
  12.4 0.6 %copy.10 = f32[16,512]{1,0:T(8,128)} copy(f32[16,512]{1,0:T(8,128)S(1)} %shard_map.73) | data formatting | bytes 65536
Async XLA Ops:
  0.0 0.9 %copy-start.5 = (f32[1,128]{1,0:T(1,128)S(1)}, f32[1,128]{1,0:T(1,128)}, u32[]{:S(2)}) copy-start(f32[1,128]{1,0:T(1,128)} %constant.2.clone.freq_hbm) | copy-start | bytes 1540
  0.0 0.9 %copy-start.4 = (s32[64]{0:T(128)S(1)}, s32[64]{0:T(128)}, u32[]{:S(2)}) copy-start(s32[64]{0:T(128)} %positions_hbm.1) | copy-start | bytes 772
  0.0 0.9 %copy-start.3 = (f32[128]{0:T(128)S(1)}, f32[128]{0:T(128)}, u32[]{:S(2)}) copy-start(f32[128]{0:T(128)} %bias_hbm.1) | copy-start | bytes 1540
  0.0 0.9 %copy-start.2 = (f32[128]{0:T(128)S(1)}, f32[128]{0:T(128)}, u32[]{:S(2)}) copy-start(f32[128]{0:T(128)} %gain_hbm.1) | copy-start | bytes 1540
  0.0 0.9 %copy-start.1 = (bf16[64,128]{1,0:T(8,128)(2,1)S(1)}, bf16[64,128]{1,0:T(8,128)(2,1)}, u32[]{:S(2)}) copy-start(bf16[64,128]{1,0:T(8,128)(2,1)} %keys_hbm.1) | copy-start | bytes 49156
  0.9 1.0 %copy-start = (bf16[64,2048]{1,0:T(8,128)(2,1)S(1)}, bf16[64,2048]{1,0:T(8,128)(2,1)}, u32[]{:S(2)}) copy-start(bf16[64,2048]{1,0:T(8,128)(2,1)} %queries_hbm.1) | copy-start | bytes 786436

commit v2 on v1

--- a/solution.py
+++ b/solution.py
@@ -181,11 +181,17 @@
     copies[5].wait()
     copies[6].wait()
     scale = 1.0 / math.sqrt(H * DH)
+    weights = scale * lax.dot_general(
+        (here == there).astype(jnp.bfloat16),
+        w_in[...],
+        (((1,), (1,)), ((), ())),
+        preferred_element_type=jnp.float32,
+    )
     for h in range(heads):
         q_rot[h * rows : (h + 1) * rows, :] = rotate(
             q_in[:, h * DH : (h + 1) * DH].astype(jnp.float32)
         ).astype(jnp.bfloat16)
-        w_wide[h] = jnp.broadcast_to(w_in[:, h : h + 1].astype(jnp.float32) * scale, (rows, DH))
+        w_wide[h] = jnp.broadcast_to(weights[:, h : h + 1], (rows, DH))
 
     row_glob = c * rows + lax.broadcasted_iota(jnp.int32, (rows, 1), 0)
     row_doc = row_glob - pos.astype(jnp.int32)
@@ -204,7 +210,9 @@
             device_id_type=MESH,
         )
 
-    def score(t, carry):
+    def score(i, carry):
+        t = chunk_end + chunk_first - 1 - i
+
         def arrive(i, carry):
             key_copy(i, c).wait_recv()
             return carry
@@ -239,7 +247,8 @@
 
     lax.fori_loop(chunk_first, chunk_end, score, 0)
 
-    def gather(t, carry):
+    def gather(i, carry):
+        t = chunk_end + chunk_first - 1 - i
         total = part_out[t, g].astype(jnp.float32)
         for d in range(1, n_head):
             part_copy(t, d).wait_recv()
@@ -278,14 +287,14 @@
         return pl.pallas_call(
             functools.partial(kernel, n_ctx, n_head, chunk),
             out_shape=jax.ShapeDtypeStruct((rows_each, tokens), jnp.float32),
-            in_specs=[pl.BlockSpec(memory_space=pl.ANY)] * 7,
+            in_specs=[pl.BlockSpec(memory_space=pltpu.HBM)] * 7,
             out_specs=pl.BlockSpec(memory_space=pltpu.VMEM),
             scratch_shapes=[
                 pltpu.VMEM(queries.shape, jnp.bfloat16),
                 pltpu.VMEM(keys.shape, jnp.bfloat16),
                 pltpu.VMEM(key_gain.shape, jnp.float32),
                 pltpu.VMEM(key_bias.shape, jnp.float32),
-                pltpu.VMEM(head_weights.shape, jnp.bfloat16),
+                pltpu.VMEM(head_weights.shape[::-1], jnp.bfloat16),
                 pltpu.VMEM(positions.shape, jnp.int32),
                 pltpu.VMEM((1, DH), jnp.float32),
                 pltpu.VMEM((heads * rows, DH), jnp.bfloat16),
@@ -300,9 +309,9 @@
                 pltpu.SemaphoreType.DMA((n_chunk, n_head - 1)),
             ],
             compiler_params=pltpu.CompilerParams(
-                collective_id=0, has_side_effects=True, vmem_limit_bytes=32 * 1024 * 1024
+                collective_id=0, has_side_effects=True, vmem_limit_bytes=60 * 1024 * 1024
             ),
-        )(queries, keys, key_gain, key_bias, head_weights, positions, jnp.asarray(freq_wide))
+        )(queries, keys, key_gain, key_bias, head_weights.T, positions, jnp.asarray(freq_wide))
 
     in_specs = (P("ctx", "head"), P("ctx", None), P(), P(), P("ctx", "head"), P("ctx"))
     out_specs = P(("ctx", "head"), None)

time: 13.2 us -> 12.4 us (0.939)
  local copies, waits for them, and re-layouts: 2.41 us -> 1.38 us
  Pallas kernels: 10.5 us -> 10.9 us
    unnamed x14 -> x1, local copies, waits for them, and re-layouts: 2.41 us -> 1.38 us
    pallas_call x1, Pallas kernels: 10.5 us -> 10.9 us  [on_device(): pl.pallas_call(functools.partial(kernel, n_ctx, n_head, chunk), out_shape...]
where the time goes in v2:
time: 12.4 us; the launch traced here: 12.3 us
  Pallas kernels  10.9 us (88%)
  local copies, waits for them, and re-layouts  1.38 us (11%)
    pallas_call x1, Pallas kernels, on_device(): pl.pallas_call(functools.partial(kernel, n_ctx, n_head, chunk), out_shape...  10.9 us
    unnamed x1, local copies, waits for them, and re-layouts  1.38 us

profile of v2, /device:TPU:9, one launch (start us, length us, event | category | flops | bytes accessed | tf_op | source)
XLA Modules:
  0.0 12.3 jit_solution(7894039221152201509)
XLA Ops:
  0.0 10.9 %shard_map.73 = f32[16,512]{1,0:T(8,128)} custom-call(bf16[64,2048]{1,0:T(8,128)(2,1)} %queries_hbm.1, bf16[64,128]{1,0:T(8,128)(2,1)} %keys_hbm.1, f32[128]{0:T(128)} %gain_hbm.1, f32[128]{0:T(128)} %bias_hbm.1, bf16[16,64]{1,0:T(8,128)(2,1)} %bitcast.1, s32[64]{0:T(128)} %positions_hbm.1, f32[1,128]{1,0:T(1,128)} %constant.2.clone.freq_hbm), custom_call_target="tpu_custom_call" | custom-call | tf_op jit(solution)/shard_map/pallas_call | solution.py:287
  10.9 1.4 %copy.9 = f32[16,512]{1,0:T(8,128)} copy(f32[16,512]{1,0:T(8,128)} %shard_map.73) | data formatting | bytes 65536

commit v3 on v2

--- a/solution.py
+++ b/solution.py
@@ -129,8 +129,8 @@
         copy.start()
     out_ref[...] = jnp.zeros_like(out_ref)
 
-    copies[0].wait()
-    copies[1].wait()
+    for copy in copies[:5]:
+        copy.wait()
     pos_wide = jnp.broadcast_to(pos_in[...].reshape(1, rows).astype(jnp.float32), (rows, rows))
     here = lax.broadcasted_iota(jnp.int32, (rows, rows), 0)
     there = lax.broadcasted_iota(jnp.int32, (rows, rows), 1)
@@ -148,8 +148,6 @@
             + pltpu.roll(values, half, 1) * sine_high
         )
 
-    for copy in copies[2:5]:
-        copy.wait()
     values = k_in[...].astype(jnp.float32)
     centered = values - jnp.mean(values, axis=-1, keepdims=True)
     spread = jnp.mean(centered * centered, axis=-1, keepdims=True)
@@ -284,6 +282,15 @@
         chunk = max(DH, tokens // 16)
         n_chunk = tokens // chunk
         rows_each = rows // n_head
+        operands = (
+            queries,
+            keys,
+            key_gain,
+            key_bias,
+            head_weights.T,
+            positions,
+            jnp.asarray(freq_wide),
+        )
         return pl.pallas_call(
             functools.partial(kernel, n_ctx, n_head, chunk),
             out_shape=jax.ShapeDtypeStruct((rows_each, tokens), jnp.float32),
@@ -309,9 +316,9 @@
                 pltpu.SemaphoreType.DMA((n_chunk, n_head - 1)),
             ],
             compiler_params=pltpu.CompilerParams(
-                collective_id=0, has_side_effects=True, vmem_limit_bytes=60 * 1024 * 1024
+                collective_id=0, has_side_effects=True, vmem_limit_bytes=32 * 1024 * 1024
             ),
-        )(queries, keys, key_gain, key_bias, head_weights.T, positions, jnp.asarray(freq_wide))
+        )(*[pltpu.with_memory_space_constraint(x, pltpu.HBM) for x in operands])
 
     in_specs = (P("ctx", "head"), P("ctx", None), P(), P(), P("ctx", "head"), P("ctx"))
     out_specs = P(("ctx", "head"), None)

time: 12.4 us -> 11.1 us (0.90)
  local copies, waits for them, and re-layouts: 1.38 us -> 0.62 us
  Pallas kernels: 10.9 us -> 10.3 us
    unnamed x1, local copies, waits for them, and re-layouts: 1.38 us -> 0.62 us
    pallas_call x1, Pallas kernels: 10.9 us -> 10.3 us  [on_device(): pl.pallas_call(functools.partial(kernel, n_ctx, n_head, chunk), out_shape...]
where the time goes in v3:
time: 11.1 us; the launch traced here: 10.9 us
  Pallas kernels  10.3 us (93%)
  local copies, waits for them, and re-layouts  0.62 us (6%)
    pallas_call x1, Pallas kernels, on_device(): pl.pallas_call(functools.partial(kernel, n_ctx, n_head, chunk), out_shape...  10.3 us
    unnamed x1, local copies, waits for them, and re-layouts  0.62 us

profile of v3, /device:TPU:9, one launch (start us, length us, event | category | flops | bytes accessed | tf_op | source)
XLA Modules:
  0.0 10.9 jit_solution(15615100387871597096)
XLA Ops:
  0.0 10.3 %shard_map.73 = f32[16,512]{1,0:T(8,128)S(1)} custom-call(bf16[64,2048]{1,0:T(8,128)(2,1)} %queries_hbm.1, bf16[64,128]{1,0:T(8,128)(2,1)} %keys_hbm.1, f32[128]{0:T(128)} %gain_hbm.1, f32[128]{0:T(128)} %bias_hbm.1, bf16[16,64]{1,0:T(8,128)(2,1)} %bitcast.1, s32[64]{0:T(128)} %positions_hbm.1, f32[1,128]{1,0:T(1,128)} %constant.2.clone.freq_hbm), custom_call_target="tpu_custom_call" | custom-call | tf_op jit(solution)/shard_map/pallas_call | solution.py:294
  10.3 0.6 %copy.9 = f32[16,512]{1,0:T(8,128)} copy(f32[16,512]{1,0:T(8,128)S(1)} %shard_map.73) | data formatting | bytes 65536

commit v4 on v3

--- a/solution.py
+++ b/solution.py
@@ -54,6 +54,13 @@
     return sine_out, cosine_out
 
 
+def partner(index, bits):
+    for b in range(bits.bit_length()):
+        if bits >> b & 1:
+            index = index + (1 - 2 * lax.rem(index // (1 << b), 2)) * (1 << b)
+    return index
+
+
 def kernel(
     n_ctx,
     n_head,
@@ -73,6 +80,7 @@
     w_in,
     pos_in,
     freq_in,
+    w_flat,
     q_rot,
     w_wide,
     k_all,
@@ -96,21 +104,6 @@
     crossing = (c + 1) * rows > first_end
     dst_end = jnp.where(crossing, n_ctx, -(-first_end // rows))
 
-    barrier = pltpu.get_barrier_semaphore()
-
-    def greet(i, carry):
-        pl.semaphore_signal(barrier, inc=1, device_id={"ctx": i, "head": g}, device_id_type=MESH)
-        return carry
-
-    lax.fori_loop(src_first, c, greet, 0)
-    for d in range(1, n_head):
-        pl.semaphore_signal(
-            barrier,
-            inc=1,
-            device_id={"ctx": c, "head": lax.rem(g + d, n_head)},
-            device_id_type=MESH,
-        )
-
     copies = [
         pltpu.make_async_copy(src, dst, in_sem.at[i])
         for i, (src, dst) in enumerate(
@@ -125,7 +118,25 @@
             ]
         )
     ]
-    for copy in copies:
+    for copy in copies[:5]:
+        copy.start()
+
+    barrier = pltpu.get_barrier_semaphore()
+
+    def greet(i, carry):
+        pl.semaphore_signal(barrier, inc=1, device_id={"ctx": i, "head": g}, device_id_type=MESH)
+        return carry
+
+    lax.fori_loop(src_first, c, greet, 0)
+    for d in range(1, n_head):
+        pl.semaphore_signal(
+            barrier,
+            inc=1,
+            device_id={"ctx": c, "head": partner(g, d)},
+            device_id_type=MESH,
+        )
+
+    for copy in copies[5:]:
         copy.start()
     out_ref[...] = jnp.zeros_like(out_ref)
 
@@ -179,17 +190,19 @@
     copies[5].wait()
     copies[6].wait()
     scale = 1.0 / math.sqrt(H * DH)
-    weights = scale * lax.dot_general(
-        (here == there).astype(jnp.bfloat16),
-        w_in[...],
-        (((1,), (1,)), ((), ())),
-        preferred_element_type=jnp.float32,
-    )
-    for h in range(heads):
-        q_rot[h * rows : (h + 1) * rows, :] = rotate(
-            q_in[:, h * DH : (h + 1) * DH].astype(jnp.float32)
-        ).astype(jnp.bfloat16)
-        w_wide[h] = jnp.broadcast_to(weights[:, h : h + 1], (rows, DH))
+    w_flat[...] = w_in[...].astype(jnp.float32) * scale
+
+    def prepare(step, carry):
+        for j in range(4):
+            h = step * 4 + j
+            q_rot[pl.ds(pl.multiple_of(h * rows, rows), rows), :] = rotate(
+                q_in[:, pl.ds(pl.multiple_of(h * DH, DH), DH)].astype(jnp.float32)
+            ).astype(jnp.bfloat16)
+            weight = jnp.where(here == there, w_flat[pl.ds(h, 1), :], 0.0)
+            w_wide[h] = jnp.broadcast_to(jnp.sum(weight, axis=1, keepdims=True), (rows, DH))
+        return carry
+
+    lax.fori_loop(0, heads // 4, prepare, 0)
 
     row_glob = c * rows + lax.broadcasted_iota(jnp.int32, (rows, 1), 0)
     row_doc = row_glob - pos.astype(jnp.int32)
@@ -198,7 +211,7 @@
     chunk_end = c // per_chunk + 1
 
     def part_copy(t, d):
-        peer = lax.rem(g + d, n_head)
+        peer = partner(g, d)
         return pltpu.make_async_remote_copy(
             src_ref=part_out.at[t, peer],
             dst_ref=part_in.at[t, d - 1],
@@ -239,7 +252,7 @@
         part = jnp.where(visible, total, 0.0).astype(jnp.bfloat16)
         for h in range(n_head):
             part_out[t, h] = part[h * rows_each : (h + 1) * rows_each, :]
-        for d in range(1, n_head):
+        for d in range(n_head - 1, 0, -1):
             part_copy(t, d).start()
         return carry
 
@@ -304,6 +317,7 @@
                 pltpu.VMEM(head_weights.shape[::-1], jnp.bfloat16),
                 pltpu.VMEM(positions.shape, jnp.int32),
                 pltpu.VMEM((1, DH), jnp.float32),
+                pltpu.VMEM((heads, rows), jnp.float32),
                 pltpu.VMEM((heads * rows, DH), jnp.bfloat16),
                 pltpu.VMEM((heads, rows, DH), jnp.float32),
                 pltpu.VMEM((tokens, DH), jnp.bfloat16),

time: 11.1 us -> 10.8 us (0.973)
  Pallas kernels: 10.3 us -> 9.98 us
    pallas_call x1, Pallas kernels: 10.3 us -> 9.98 us  [on_device(): pl.pallas_call(functools.partial(kernel, n_ctx, n_head, chunk), out_shape...]
where the time goes in v4:
time: 10.8 us; the launch traced here: 10.6 us
  Pallas kernels  9.98 us (92%)
  local copies, waits for them, and re-layouts  0.62 us (6%)
    pallas_call x1, Pallas kernels, on_device(): pl.pallas_call(functools.partial(kernel, n_ctx, n_head, chunk), out_shape...  9.98 us
    unnamed x1, local copies, waits for them, and re-layouts  0.62 us

profile of v4, /device:TPU:9, one launch (start us, length us, event | category | flops | bytes accessed | tf_op | source)
XLA Modules:
  0.0 10.6 jit_solution(13401851480664613904)
XLA Ops:
  0.0 10.0 %shard_map.73 = f32[16,512]{1,0:T(8,128)S(1)} custom-call(bf16[64,2048]{1,0:T(8,128)(2,1)} %queries_hbm.1, bf16[64,128]{1,0:T(8,128)(2,1)} %keys_hbm.1, f32[128]{0:T(128)} %gain_hbm.1, f32[128]{0:T(128)} %bias_hbm.1, bf16[16,64]{1,0:T(8,128)(2,1)} %bitcast.1, s32[64]{0:T(128)} %positions_hbm.1, f32[1,128]{1,0:T(1,128)} %constant.2.clone.freq_hbm), custom_call_target="tpu_custom_call" | custom-call | tf_op jit(solution)/shard_map/pallas_call | solution.py:307
  10.0 0.6 %copy.9 = f32[16,512]{1,0:T(8,128)} copy(f32[16,512]{1,0:T(8,128)S(1)} %shard_map.73) | data formatting | bytes 65536

commit v5 on v4

--- a/solution.py
+++ b/solution.py
@@ -182,7 +182,7 @@
         )
 
     def send_keys(i, carry):
-        key_copy(c, dst_end + c - i).start()
+        key_copy(c, jnp.where(i + 1 < dst_end, i + 1, c + 1)).start()
         return carry
 
     lax.fori_loop(c + 1, dst_end, send_keys, 0)
@@ -192,9 +192,11 @@
     scale = 1.0 / math.sqrt(H * DH)
     w_flat[...] = w_in[...].astype(jnp.float32) * scale
 
+    unroll = math.gcd(heads, 8)
+
     def prepare(step, carry):
-        for j in range(4):
-            h = step * 4 + j
+        for j in range(unroll):
+            h = step * unroll + j
             q_rot[pl.ds(pl.multiple_of(h * rows, rows), rows), :] = rotate(
                 q_in[:, pl.ds(pl.multiple_of(h * DH, DH), DH)].astype(jnp.float32)
             ).astype(jnp.bfloat16)
@@ -202,7 +204,7 @@
             w_wide[h] = jnp.broadcast_to(jnp.sum(weight, axis=1, keepdims=True), (rows, DH))
         return carry
 
-    lax.fori_loop(0, heads // 4, prepare, 0)
+    lax.fori_loop(0, heads // unroll, prepare, 0)
 
     row_glob = c * rows + lax.broadcasted_iota(jnp.int32, (rows, 1), 0)
     row_doc = row_glob - pos.astype(jnp.int32)

time: 10.8 us -> 10.8 us (level)
  no operation moved by 1% of the time
where the time goes in v5:
time: 10.8 us; the launch traced here: 10.6 us
  Pallas kernels  9.98 us (92%)
  local copies, waits for them, and re-layouts  0.62 us (6%)
    pallas_call x1, Pallas kernels, on_device(): pl.pallas_call(functools.partial(kernel, n_ctx, n_head, chunk), out_shape...  9.98 us
    unnamed x1, local copies, waits for them, and re-layouts  0.62 us

profile of v5, /device:TPU:9, one launch (start us, length us, event | category | flops | bytes accessed | tf_op | source)
XLA Modules:
  0.0 10.6 jit_solution(6199480838860820199)
XLA Ops:
  0.0 10.0 %shard_map.73 = f32[16,512]{1,0:T(8,128)S(1)} custom-call(bf16[64,2048]{1,0:T(8,128)(2,1)} %queries_hbm.1, bf16[64,128]{1,0:T(8,128)(2,1)} %keys_hbm.1, f32[128]{0:T(128)} %gain_hbm.1, f32[128]{0:T(128)} %bias_hbm.1, bf16[16,64]{1,0:T(8,128)(2,1)} %bitcast.1, s32[64]{0:T(128)} %positions_hbm.1, f32[1,128]{1,0:T(1,128)} %constant.2.clone.freq_hbm), custom_call_target="tpu_custom_call" | custom-call | tf_op jit(solution)/shard_map/pallas_call | solution.py:309
  10.0 0.6 %copy.9 = f32[16,512]{1,0:T(8,128)} copy(f32[16,512]{1,0:T(8,128)S(1)} %shard_map.73) | data formatting | bytes 65536

commit v6 on v5

--- a/solution.py
+++ b/solution.py
@@ -182,7 +182,7 @@
         )
 
     def send_keys(i, carry):
-        key_copy(c, jnp.where(i + 1 < dst_end, i + 1, c + 1)).start()
+        key_copy(c, i).start()
         return carry
 
     lax.fori_loop(c + 1, dst_end, send_keys, 0)

time: 10.8 us -> 10.7 us (level)
  the two profiles are of different devices: /device:TPU:9 before, /device:TPU:18 now
where the time goes in v6:
time: 10.7 us; the launch traced here: 10.5 us
  Pallas kernels  9.9 us (93%)
  local copies, waits for them, and re-layouts  0.62 us (6%)
    pallas_call x1, Pallas kernels, on_device(): pl.pallas_call(functools.partial(kernel, n_ctx, n_head, chunk), out_shape...  9.9 us
    unnamed x1, local copies, waits for them, and re-layouts  0.62 us

profile of v6, /device:TPU:18, one launch (start us, length us, event | category | flops | bytes accessed | tf_op | source)
XLA Modules:
  0.0 10.5 jit_solution(12094949340681562407)
XLA Ops:
  0.0 9.9 %shard_map.73 = f32[16,512]{1,0:T(8,128)S(1)} custom-call(bf16[64,2048]{1,0:T(8,128)(2,1)} %queries_hbm.1, bf16[64,128]{1,0:T(8,128)(2,1)} %keys_hbm.1, f32[128]{0:T(128)} %gain_hbm.1, f32[128]{0:T(128)} %bias_hbm.1, bf16[16,64]{1,0:T(8,128)(2,1)} %bitcast.1, s32[64]{0:T(128)} %positions_hbm.1, f32[1,128]{1,0:T(1,128)} %constant.2.clone.freq_hbm), custom_call_target="tpu_custom_call" | custom-call | tf_op jit(solution)/shard_map/pallas_call | solution.py:309
  9.9 0.6 %copy.9 = f32[16,512]{1,0:T(8,128)} copy(f32[16,512]{1,0:T(8,128)S(1)} %shard_map.73) | data formatting | bytes 65536
